TPU v7x, 128 devices: a whole 4x4x4 slice. The times are simulated.
128 devices in a mesh: ctx: 32 (over z_hi, x, y), fsdp: 4 (over z_lo, core).
Axes of the slice: x: 4, y: 4, z: 4 (z_hi: 2, z_lo: 2; z = z_hi * 2 + z_lo), core: 2. Of those that a mesh axis runs over, the one named last changes fastest.
Arguments:
- tokens: bfloat16 [4, 4096, 960], P('fsdp', 'ctx'), may hold values from -6 to 6
- block_pairs: int32 [4, 32], P('fsdp'), may hold values from 0 to 31, each once within a row
- w_query: bfloat16 [960, 960], P('fsdp'), may hold values from -0.375 to 0.375
- key_weight: bfloat16 [960, 320], P('fsdp'), may hold values from -0.1875 to 0.1875
- value_weight: bfloat16 [960, 320], P('fsdp'), may hold values from -0.1875 to 0.1875
- w_out: bfloat16 [960, 960], P('fsdp'), may hold values from -0.75 to 0.75
- gain_attn: bfloat16 [960], P('fsdp'), may hold values from 0.25 to 1.75
- gain_mlp: bfloat16 [960], P('fsdp'), may hold values from 0.25 to 1.75
- w_gate: bfloat16 [960, 2560], P(None, 'fsdp'), may hold values from -0.1875 to 0.1875
- w_up: bfloat16 [960, 2560], P(None, 'fsdp'), may hold values from -0.1875 to 0.1875
- w_down: bfloat16 [2560, 960], P('fsdp'), may hold values from -0.25 to 0.25
- cotangent: bfloat16 [4, 4096, 960], P('fsdp', 'ctx'), may hold values from -6 to 6
Outputs:
- result: bfloat16 [4, 4096, 960], P('fsdp', 'ctx')
- input_grad: float32 [4, 4096, 960], P('fsdp', 'ctx')
- grad_query: float32 [960, 960], P('fsdp')
- grad_key: float32 [960, 320], P('fsdp')
- grad_value: float32 [960, 320], P('fsdp')
- grad_out: float32 [960, 960], P('fsdp')
- grad_gain_attn: float32 [960], P('fsdp')
- grad_gain_mlp: float32 [960], P('fsdp')
- grad_gate: float32 [960, 2560], P(None, 'fsdp')
- grad_up: float32 [960, 2560], P(None, 'fsdp')
- grad_down: float32 [2560, 960], P('fsdp')
Inputs may be any that keep to these rules, and one draw needn't show every extreme that they name: Each row is a permutation; the index c of ctx holds, for that row's sequence, the position blocks block_pairs[s, c] and 63 - block_pairs[s, c], each of 64 positions, in that order.
All inputs are finite; a program needn't handle non-finite values.
Results may differ from a plain program's by a relative error of at most 0.03.
Values may be sent and summed in bfloat16 or wider, within the bound.
No kernel may reach another device: no remote copies, remote signals or barrier semaphores. Data moves between devices by JAX's collectives and lax.ppermute only.
A program may use at most 128 MiB of HBM per device.

v0:
```python
import jax
import jax.numpy as jnp
from jax import lax
from jax.sharding import PartitionSpec as P

QUERY_HEADS = 15
KEY_VALUE_HEADS = 5
HEAD_SIZE = 64


EPSILON = 1e-05


def matrix_product(left, right):
    return jnp.dot(left, right, preferred_element_type=jnp.float32)


def left_inner(left, right):
    return lax.dot_general(
        left, right, (((0,), (0,)), ((), ())), preferred_element_type=jnp.float32
    )


def right_inner(left, right):
    return lax.dot_general(
        left, right, (((1,), (1,)), ((), ())), preferred_element_type=jnp.float32
    )


def apply_rotation(values, cosine_table, sinusoid_table):
    half_width = values.shape[-1] // 2
    leading = values[..., :half_width]
    trailing = values[..., half_width:]
    return jnp.concatenate(
        [
            leading * cosine_table - trailing * sinusoid_table,
            trailing * cosine_table + leading * sinusoid_table,
        ],
        axis=-1,
    )


def reverse_rotation(gradient, cosine_table, sinusoid_table):
    half_width = gradient.shape[-1] // 2
    leading = gradient[..., :half_width]
    trailing = gradient[..., half_width:]
    return jnp.concatenate(
        [
            leading * cosine_table + trailing * sinusoid_table,
            trailing * cosine_table - leading * sinusoid_table,
        ],
        axis=-1,
    )


def norm_forward(values, gain_vector):
    inverse = lax.rsqrt(jnp.mean(values * values, axis=-1, keepdims=True) + EPSILON)
    return (values * inverse * gain_vector, inverse)


def norm_backward(values, inverse, gain_vector, gradient):
    weighted = gradient * gain_vector
    through = inverse * weighted - values * inverse**3 * jnp.mean(
        weighted * values, axis=-1, keepdims=True
    )
    return (through, jnp.sum(gradient * values * inverse, axis=0))


def pair_positions(pair_rows, count, span):
    block_list = jnp.stack([pair_rows, 2 * count - 1 - pair_rows], axis=-1)
    offsets = jnp.arange(span, dtype=jnp.int32)
    return (block_list[..., None] * span + offsets).reshape(pair_rows.shape[:-1] + (-1,))


def masked_scores(query_rows, key_block, query_places, key_places, factor):
    scores = (
        jnp.einsum("qkgd,skd->kgqs", query_rows, key_block, preferred_element_type=jnp.float32)
        * factor
    )
    allowed = query_places[:, None] >= key_places[None, :]
    return jnp.where(allowed[None, None], scores, -1e30)


def split_blocks(rows_of_key, rows_of_value, key_places):
    key_count = rows_of_key.shape[0]
    rows_per_block = min(512, key_count)
    count_blocks = key_count // rows_per_block
    return (
        rows_of_key.reshape((count_blocks, rows_per_block) + rows_of_key.shape[1:]),
        rows_of_value.reshape((count_blocks, rows_per_block) + rows_of_value.shape[1:]),
        key_places.reshape(count_blocks, rows_per_block),
    )


def attention_forward(query_rows, rows_of_key, rows_of_value, query_places, key_places, factor):
    key_blocks, value_blocks, place_blocks = split_blocks(rows_of_key, rows_of_value, key_places)
    shape_stat = (query_rows.shape[1], query_rows.shape[2], query_rows.shape[0])
    start_max = jnp.full(shape_stat, -1e30, jnp.float32)
    start_sum = jnp.zeros(shape_stat, jnp.float32)

    def statistics(running, block_item):
        running_max, running_sum = running
        key_block, key_place = block_item
        scores = masked_scores(query_rows, key_block, query_places, key_place, factor)
        new_max = jnp.maximum(running_max, jnp.max(scores, axis=-1))
        running_sum = running_sum * jnp.exp(running_max - new_max) + jnp.sum(
            jnp.exp(scores - new_max[..., None]), axis=-1
        )
        return ((new_max, running_sum), None)

    (row_max, row_sum), leftover = lax.scan(
        statistics, (start_max, start_sum), (key_blocks, place_blocks)
    )
    log_total = row_max + jnp.log(row_sum)

    def accumulate(running, block_item):
        key_block, value_block, key_place = block_item
        scores = masked_scores(query_rows, key_block, query_places, key_place, factor)
        soft_weights = jnp.exp(scores - log_total[..., None]).astype(jnp.bfloat16)
        return (
            running
            + jnp.einsum(
                "kgqs,skd->qkgd", soft_weights, value_block, preferred_element_type=jnp.float32
            ),
            None,
        )

    attended, leftover = lax.scan(
        accumulate,
        jnp.zeros(query_rows.shape, jnp.float32),
        (key_blocks, value_blocks, place_blocks),
    )
    return (attended, log_total)


def attention_backward(
    query_rows,
    rows_of_key,
    rows_of_value,
    query_places,
    key_places,
    factor,
    attended,
    log_total,
    attended_gradient,
):
    key_blocks, value_blocks, place_blocks = split_blocks(rows_of_key, rows_of_value, key_places)
    row_delta = jnp.transpose(
        jnp.sum(attended_gradient.astype(jnp.float32) * attended, axis=-1), (1, 2, 0)
    )

    def backward_block(running, block_item):
        key_block, value_block, key_place = block_item
        scores = masked_scores(query_rows, key_block, query_places, key_place, factor)
        soft_weights = jnp.exp(scores - log_total[..., None])
        grad_soft = jnp.einsum(
            "qkgd,skd->kgqs", attended_gradient, value_block, preferred_element_type=jnp.float32
        )
        grad_scores = (soft_weights * (grad_soft - row_delta[..., None])).astype(jnp.bfloat16)
        running = running + jnp.einsum(
            "kgqs,skd->qkgd", grad_scores, key_block, preferred_element_type=jnp.float32
        )
        grad_key_block = (
            jnp.einsum(
                "kgqs,qkgd->skd", grad_scores, query_rows, preferred_element_type=jnp.float32
            )
            * factor
        )
        grad_value_block = jnp.einsum(
            "kgqs,qkgd->skd",
            soft_weights.astype(jnp.bfloat16),
            attended_gradient,
            preferred_element_type=jnp.float32,
        )
        return (running, (grad_key_block, grad_value_block))

    grad_queries, (grad_key_rows, grad_value_rows) = lax.scan(
        backward_block,
        jnp.zeros(query_rows.shape, jnp.float32),
        (key_blocks, value_blocks, place_blocks),
    )
    return (
        grad_queries * factor,
        grad_key_rows.reshape(rows_of_key.shape),
        grad_value_rows.reshape(rows_of_value.shape),
    )


def body(
    tokens,
    block_pairs,
    w_query,
    key_weight,
    value_weight,
    w_out,
    gain_attn,
    gain_mlp,
    w_gate,
    w_up,
    w_down,
    cotangent,
):
    sequence_count, resident_rows, width_model = tokens.shape
    ctx_count = lax.axis_size("ctx")
    ctx_here = lax.axis_index("ctx")
    span = resident_rows // 2
    every_row_set = sequence_count * resident_rows
    query_group_width = QUERY_HEADS // KEY_VALUE_HEADS
    factor = HEAD_SIZE ** (-0.5)
    full_query, complete_key, full_value, full_out, full_gain_attn, full_gain_mlp = (
        lax.all_gather(w_query, "fsdp", axis=0, tiled=True),
        lax.all_gather(key_weight, "fsdp", axis=0, tiled=True),
        lax.all_gather(value_weight, "fsdp", axis=0, tiled=True),
        lax.all_gather(w_out, "fsdp", axis=0, tiled=True),
        lax.all_gather(gain_attn, "fsdp", axis=0, tiled=True),
        lax.all_gather(gain_mlp, "fsdp", axis=0, tiled=True),
    )
    gain_one = full_gain_attn.astype(jnp.float32)
    gain_two = full_gain_mlp.astype(jnp.float32)
    inputs = tokens.reshape(every_row_set, width_model).astype(jnp.float32)
    upstream = cotangent.reshape(every_row_set, width_model).astype(jnp.float32)
    own_pairs = lax.dynamic_slice_in_dim(block_pairs, ctx_here, 1, axis=1)
    query_places = pair_positions(own_pairs, ctx_count, span)
    key_places = pair_positions(block_pairs, ctx_count, span)
    frequency = 10000.0 ** (-jnp.arange(HEAD_SIZE // 2, dtype=jnp.float32) / (HEAD_SIZE // 2))
    angles = query_places.reshape(every_row_set).astype(jnp.float32)[:, None] * frequency[None, :]
    cosine_table = jnp.cos(angles)[:, None, :]
    sinusoid_table = jnp.sin(angles)[:, None, :]
    normed_one, inverse_one = norm_forward(inputs, gain_one)
    normalized_reduced = normed_one.astype(jnp.bfloat16)
    query_matrix = apply_rotation(
        matrix_product(normalized_reduced, full_query).reshape(
            every_row_set, QUERY_HEADS, HEAD_SIZE
        ),
        cosine_table,
        sinusoid_table,
    ).astype(jnp.bfloat16)
    resident_key = apply_rotation(
        matrix_product(normalized_reduced, complete_key).reshape(
            every_row_set, KEY_VALUE_HEADS, HEAD_SIZE
        ),
        cosine_table,
        sinusoid_table,
    ).astype(jnp.bfloat16)
    resident_value = matrix_product(normalized_reduced, full_value).astype(jnp.bfloat16)
    gathered_keys, gathered_values = (
        lax.all_gather(
            resident_key.reshape(sequence_count, resident_rows, KEY_VALUE_HEADS * HEAD_SIZE),
            "ctx",
            axis=1,
            tiled=True,
        ),
        lax.all_gather(
            resident_value.reshape(sequence_count, resident_rows, KEY_VALUE_HEADS * HEAD_SIZE),
            "ctx",
            axis=1,
            tiled=True,
        ),
    )
    grouped_queries = query_matrix.reshape(
        sequence_count, resident_rows, KEY_VALUE_HEADS, query_group_width, HEAD_SIZE
    )
    heads_of_key = gathered_keys.reshape(sequence_count, -1, KEY_VALUE_HEADS, HEAD_SIZE)
    heads_of_value = gathered_values.reshape(sequence_count, -1, KEY_VALUE_HEADS, HEAD_SIZE)
    sequence = 0
    attended, log_total = attention_forward(
        grouped_queries[sequence],
        heads_of_key[sequence],
        heads_of_value[sequence],
        query_places[sequence],
        key_places[sequence],
        factor,
    )
    attended_list = [attended]
    log_list = [log_total]
    attended_all = jnp.stack(attended_list)
    attended_low = attended_all.reshape(every_row_set, QUERY_HEADS * HEAD_SIZE).astype(jnp.bfloat16)
    middle = inputs + matrix_product(attended_low, full_out)
    normed_two, inverse_two = norm_forward(middle, gain_two)
    normed_mlp = normed_two.astype(jnp.bfloat16)
    gate_w, up_w, down_w = (
        lax.all_gather(w_gate, "fsdp", axis=1, tiled=True),
        lax.all_gather(w_up, "fsdp", axis=1, tiled=True),
        lax.all_gather(w_down, "fsdp", axis=0, tiled=True),
    )
    gate_pre = matrix_product(normed_mlp, gate_w)
    up_pre = matrix_product(normed_mlp, up_w)
    sigmoid_gate = jax.nn.sigmoid(gate_pre)
    hidden = (gate_pre * sigmoid_gate * up_pre).astype(jnp.bfloat16)
    mlp_term = matrix_product(hidden, down_w)
    result = (
        (middle + mlp_term).astype(jnp.bfloat16).reshape(sequence_count, resident_rows, width_model)
    )
    grad_mlp = upstream.astype(jnp.bfloat16)
    grad_hidden = right_inner(grad_mlp, down_w)
    grad_down_w = left_inner(hidden, grad_mlp)
    grad_up_pre = (grad_hidden * gate_pre * sigmoid_gate).astype(jnp.bfloat16)
    grad_gate_pre = (
        grad_hidden * up_pre * sigmoid_gate * (1.0 + gate_pre * (1.0 - sigmoid_gate))
    ).astype(jnp.bfloat16)
    grad_gate_w = left_inner(normed_mlp, grad_gate_pre)
    grad_up_w = left_inner(normed_mlp, grad_up_pre)
    grad_normed_two = right_inner(grad_gate_pre, gate_w) + right_inner(grad_up_pre, up_w)
    through_two, grad_gain_two = norm_backward(middle, inverse_two, gain_two, grad_normed_two)
    grad_middle = upstream + through_two
    grad_branch = grad_middle.astype(jnp.bfloat16)
    attended_gradient = right_inner(grad_branch, full_out).astype(jnp.bfloat16)
    grad_out_w = left_inner(attended_low, grad_branch)
    grouped_gradient = attended_gradient.reshape(
        sequence_count, resident_rows, KEY_VALUE_HEADS, query_group_width, HEAD_SIZE
    )
    sequence = 0
    grad_queries, key_gradients, value_gradients = attention_backward(
        grouped_queries[sequence],
        heads_of_key[sequence],
        heads_of_value[sequence],
        query_places[sequence],
        key_places[sequence],
        factor,
        attended_list[sequence],
        log_list[sequence],
        grouped_gradient[sequence],
    )
    query_grad_list = [grad_queries]
    key_gradient_items = [key_gradients.reshape(-1, KEY_VALUE_HEADS * HEAD_SIZE)]
    value_gradient_items = [value_gradients.reshape(-1, KEY_VALUE_HEADS * HEAD_SIZE)]
    own_key_gradient, own_value_gradient = (
        lax.psum_scatter(
            jnp.stack(key_gradient_items).astype(jnp.bfloat16),
            "ctx",
            scatter_dimension=1,
            tiled=True,
        ).astype(jnp.float32),
        lax.psum_scatter(
            jnp.stack(value_gradient_items).astype(jnp.bfloat16),
            "ctx",
            scatter_dimension=1,
            tiled=True,
        ).astype(jnp.float32),
    )
    grad_query_pre = (
        reverse_rotation(
            jnp.stack(query_grad_list).reshape(every_row_set, QUERY_HEADS, HEAD_SIZE),
            cosine_table,
            sinusoid_table,
        )
        .reshape(every_row_set, QUERY_HEADS * HEAD_SIZE)
        .astype(jnp.bfloat16)
    )
    grad_key_pre = (
        reverse_rotation(
            own_key_gradient.reshape(every_row_set, KEY_VALUE_HEADS, HEAD_SIZE),
            cosine_table,
            sinusoid_table,
        )
        .reshape(every_row_set, KEY_VALUE_HEADS * HEAD_SIZE)
        .astype(jnp.bfloat16)
    )
    value_gradient_prior = own_value_gradient.reshape(
        every_row_set, KEY_VALUE_HEADS * HEAD_SIZE
    ).astype(jnp.bfloat16)
    grad_query_w = left_inner(normalized_reduced, grad_query_pre)
    grad_key_w = left_inner(normalized_reduced, grad_key_pre)
    grad_value_w = left_inner(normalized_reduced, value_gradient_prior)
    grad_normed_one = (
        right_inner(grad_query_pre, full_query)
        + right_inner(grad_key_pre, complete_key)
        + right_inner(value_gradient_prior, full_value)
    )
    through_one, grad_gain_one = norm_backward(inputs, inverse_one, gain_one, grad_normed_one)
    input_grad = (grad_middle + through_one).reshape(sequence_count, resident_rows, width_model)
    (
        shard_query,
        shard_key,
        shard_value,
        shard_out,
        shard_gain_one,
        shard_gain_two,
        shard_gate,
        shard_up,
        shard_down,
    ) = (
        lax.psum_scatter(
            grad_query_w.astype(jnp.bfloat16), "fsdp", scatter_dimension=0, tiled=True
        ).astype(jnp.float32),
        lax.psum_scatter(
            grad_key_w.astype(jnp.bfloat16), "fsdp", scatter_dimension=0, tiled=True
        ).astype(jnp.float32),
        lax.psum_scatter(
            grad_value_w.astype(jnp.bfloat16), "fsdp", scatter_dimension=0, tiled=True
        ).astype(jnp.float32),
        lax.psum_scatter(
            grad_out_w.astype(jnp.bfloat16), "fsdp", scatter_dimension=0, tiled=True
        ).astype(jnp.float32),
        lax.psum_scatter(
            grad_gain_one.astype(jnp.bfloat16), "fsdp", scatter_dimension=0, tiled=True
        ).astype(jnp.float32),
        lax.psum_scatter(
            grad_gain_two.astype(jnp.bfloat16), "fsdp", scatter_dimension=0, tiled=True
        ).astype(jnp.float32),
        lax.psum_scatter(
            grad_gate_w.astype(jnp.bfloat16), "fsdp", scatter_dimension=1, tiled=True
        ).astype(jnp.float32),
        lax.psum_scatter(
            grad_up_w.astype(jnp.bfloat16), "fsdp", scatter_dimension=1, tiled=True
        ).astype(jnp.float32),
        lax.psum_scatter(
            grad_down_w.astype(jnp.bfloat16), "fsdp", scatter_dimension=0, tiled=True
        ).astype(jnp.float32),
    )
    summed = (
        lax.psum(shard_query.astype(jnp.bfloat16), "ctx").astype(jnp.float32),
        lax.psum(shard_key.astype(jnp.bfloat16), "ctx").astype(jnp.float32),
        lax.psum(shard_value.astype(jnp.bfloat16), "ctx").astype(jnp.float32),
        lax.psum(shard_out.astype(jnp.bfloat16), "ctx").astype(jnp.float32),
        lax.psum(shard_gain_one.astype(jnp.bfloat16), "ctx").astype(jnp.float32),
        lax.psum(shard_gain_two.astype(jnp.bfloat16), "ctx").astype(jnp.float32),
        lax.psum(shard_gate.astype(jnp.bfloat16), "ctx").astype(jnp.float32),
        lax.psum(shard_up.astype(jnp.bfloat16), "ctx").astype(jnp.float32),
        lax.psum(shard_down.astype(jnp.bfloat16), "ctx").astype(jnp.float32),
    )
    return (
        result,
        input_grad,
        summed[0],
        summed[1],
        summed[2],
        summed[3],
        summed[4],
        summed[5],
        summed[6],
        summed[7],
        summed[8],
    )


def solution(mesh):
    in_specs = (
        P("fsdp", "ctx", None),
        P("fsdp", None),
        P("fsdp", None),
        P("fsdp", None),
        P("fsdp", None),
        P("fsdp", None),
        P("fsdp"),
        P("fsdp"),
        P(None, "fsdp"),
        P(None, "fsdp"),
        P("fsdp", None),
        P("fsdp", "ctx", None),
    )
    out_specs = (
        P("fsdp", "ctx", None),
        P("fsdp", "ctx", None),
        P("fsdp", None),
        P("fsdp", None),
        P("fsdp", None),
        P("fsdp", None),
        P("fsdp"),
        P("fsdp"),
        P(None, "fsdp"),
        P(None, "fsdp"),
        P("fsdp", None),
    )
    return jax.shard_map(body, mesh=mesh, in_specs=in_specs, out_specs=out_specs, check_vma=False)
```

profile of v0, /device:TPU:0, one launch (start us, length us, event | category | flops | bytes accessed | tf_op | source)
XLA Modules:
  0.0 1669.8 jit_solution(8107240454076885623)
XLA Ops:
  8.0 8.6 all-gather.1
  19.6 7.1 all-reduce.7
  28.0 11.5 all-gather.2
  51.1 79.9 %all-gather.23.cloned.1.call-done = bf16[4096,320]{0,1:T(8,128)(2,1)} async-done(((bf16[128,320]{0,1:T(8,128)(2,1)}), bf16[4096,320]{0,1:T(8,128)(2,1)}) %all-gather.23.cloned.1.call-update) | async-done | bytes 2621456 | tf_op jit(solution)/shard_map/all_gather | solution.py:253
  136.2 79.3 %all-gather.11.cloned.1.call-done = bf16[1,4096,320]{1,2,0:T(8,128)(2,1)} async-done(((bf16[1,128,320]{1,2,0:T(8,128)(2,1)}), bf16[1,4096,320]{1,2,0:T(8,128)(2,1)}) %all-gather.11.cloned.1.call-update) | async-done | bytes 2621456 | tf_op jit(solution)/shard_map/all_gather | solution.py:247
  219.3 47.8 %while.39 = (s32[]{:T(128)}, f32[5,3,128]{2,1,0:T(4,128)S(1)}, f32[5,3,128]{2,1,0:T(4,128)S(1)}, s32[8,512]{1,0:T(8,128)S(1)}, bf16[8,512,5,64]{1,3,2,0:T(8,128)...) while((s32[]{:T(128)}, f32[5,3,128]{2,1,0:T(4,128)S(1)}, ...), condition=%wide.region_4.5_spmd.clone, body=%wide.region_1.4_spmd.clone.sunk | while | flops 132785664 | bytes 8742528 | solution.py:111
  267.2 28.8 %while.40 = (s32[]{:T(128)}, f32[128,5,3,64]{0,3,2,1:T(8,128)}, bf16[8,512,5,64]{1,3,2,0:T(8,128)(2,1)}, s32[8,512]{1,0:T(8,128)S(1)}, bf16[8,512,5,64]{1,3,2,0:...) while((s32[]{:T(128)}, f32[128,5,3,64]{0,3,2,1:T(8,128)}, ...), condition=%wide.region_6.7_spmd.clone, body=%wide.region_5.6_spmd.clone.sunk | while | flops 255901824 | bytes 2035330 | solution.py:128
  300.7 4.3 fusion.105
  305.0 48.2 %all-gather.19.cloned.1.call-done = bf16[960,2560]{1,0:T(8,128)(2,1)} async-done(((bf16[960,640]{1,0:T(8,128)(2,1)}), bf16[960,2560]{1,0:T(8,128)(2,1)}) %all-gather.19.cloned.1.call-update) | async-done | bytes 4915216 | tf_op jit(solution)/shard_map/all_gather | solution.py:283
  353.2 4.3 fusion.106
  357.5 50.9 %all-gather.21.cloned.1.call-done = bf16[2560,960]{0,1:T(8,128)(2,1)} async-done(((bf16[640,960]{0,1:T(8,128)(2,1)}), bf16[2560,960]{0,1:T(8,128)(2,1)}) %all-gather.21.cloned.1.call-update) | async-done | bytes 4915216 | tf_op jit(solution)/shard_map/all_gather | solution.py:284
  408.4 5.5 multiply_convert_fusion
  413.9 4.3 fusion.107
  421.6 93.8 %while.41 = (s32[]{:T(128)}, f32[128,5,3,64]{0,3,2,1:T(8,128)}, bf16[8,512,5,64]{1,3,2,0:T(8,128)(2,1)}, bf16[8,512,5,64]{1,3,2,0:T(8,128)(2,1)}, bf16[8,512,5,6...) while((s32[]{:T(128)}, f32[128,5,3,64]{0,3,2,1:T(8,128)}, ...), condition=%wide.region_11.12_spmd.clone, body=%wide.region_10.11_spmd.clone.sunk | while | flops 639451264 | bytes 63798108 | solution.py:177
  522.2 14.3 copy.73
  536.5 5.0 copy.94
  548.0 14.3 copy.75
  562.3 5.0 copy.93
  567.4 201.8 %reduce-scatter.28.cloned.1.call-done = bf16[128,320]{1,0:T(8,128)(2,1)} async-done(((bf16[4096,320]{1,0:T(8,128)(2,1)}), bf16[128,320]{1,0:T(8,128)(2,1)}) %reduce-scatter.28.cloned.1.call-update) | async-done | bytes 81936
  772.2 225.9 %reduce-scatter.30.cloned.1.call-done = bf16[128,320]{1,0:T(8,128)(2,1)} async-done(((bf16[4096,320]{1,0:T(8,128)(2,1)}), bf16[128,320]{1,0:T(8,128)(2,1)}) %reduce-scatter.30.cloned.1.call-update) | async-done | bytes 81936
  1004.5 7.9 copy.81
  1017.1 7.9 copy.83
  1029.8 7.8 copy.85
  1046.6 50.8 %reduce-scatter.36.cloned.1.call-done = bf16[640,960]{1,0:T(8,128)(2,1)} async-done(((bf16[2560,960]{1,0:T(8,128)(2,1)}), bf16[640,960]{1,0:T(8,128)(2,1)}) %reduce-scatter.36.cloned.1.call-update) | async-done | bytes 1228816
  1099.8 55.0 %reduce-scatter.38.cloned.1.call-done = bf16[640,960]{1,0:T(8,128)(2,1)} async-done(((bf16[2560,960]{1,0:T(8,128)(2,1)}), bf16[640,960]{1,0:T(8,128)(2,1)}) %reduce-scatter.38.cloned.1.call-update) | async-done | bytes 1228816
  1157.2 54.8 %reduce-scatter.40.cloned.1.call-done = bf16[640,960]{1,0:T(8,128)(2,1)} async-done(((bf16[2560,960]{1,0:T(8,128)(2,1)}), bf16[640,960]{1,0:T(8,128)(2,1)}) %reduce-scatter.40.cloned.1.call-update) | async-done | bytes 1228816
  1214.4 28.7 %reduce-scatter.24.cloned.1.call-done = bf16[240,960]{1,0:T(8,128)(2,1)} async-done(((bf16[960,960]{1,0:T(8,128)(2,1)}), bf16[240,960]{1,0:T(8,128)(2,1)}) %reduce-scatter.24.cloned.1.call-update) | async-done | bytes 460816 | tf_op jit(solution)/shard_map/reduce_scatter | solution.py:383
  1243.1 31.1 %reduce-scatter.26.cloned.1.call-done = bf16[240,960]{1,0:T(8,128)(2,1)} async-done(((bf16[960,960]{1,0:T(8,128)(2,1)}), bf16[240,960]{1,0:T(8,128)(2,1)}) %reduce-scatter.26.cloned.1.call-update) | async-done | bytes 460816 | tf_op jit(solution)/shard_map/reduce_scatter | solution.py:392
  1274.8 4.6 fusion.60
  1281.8 5.8 all-reduce.6
  1287.7 96.5 %all-reduce.4 = (bf16[240]{0:T(256)(128)(2,1)S(1)}, bf16[240]{0:T(256)(128)(2,1)S(1)}) all-reduce(bf16[240]{0:T(256)(128)(2,1)S(1)} %dynamic-slice.3, bf16[240]{0:T(256)(128)(2,1)S(1)} %dynamic-slice.5), channel_id=1, replica_groups=mesh['ctx'=32,'fsdp'=4] {'ctx'}, use_global_device_ids=true, to_apply=%region_25.26 | all-reduce | flops 480 | bytes 1920 | tf_op jit(solution)/shard_map/psum | solution.py:416
  1386.3 265.2 %all-reduce.10.cloned.1.call-done = (bf16[240,960]{1,0:T(8,128)(2,1)}, bf16[240,320]{0,1:T(8,128)(2,1)}, bf16[240,320]{0,1:T(8,128)(2,1)}, bf16[240,960]{1,0:T(8...) async-done(((bf16[240,960]{1,0:T(8,128)(2,1)}, bf16[240,320]{0,1:T(8,128)(2,1)}, bf16[240,320]{0,1:T(8,128)(2,1)}, ...) | async-done | bytes 4915216 | tf_op jit(solution)/shard_map/psum | solution.py:412
  (486 shorter events, 266.1 us)
Async XLA Ops:
  7.2 10.5 copy-start.36
  7.2 11.9 copy-start.38
  7.2 12.1 copy-start.39
  7.2 19.5 %copy-start.3 = (bf16[1,128,960]{1,2,0:T(8,128)(2,1)S(1)}, bf16[1,128,960]{1,2,0:T(8,128)(2,1)}, u32[]{:S(2)}) copy-start(bf16[1,128,960]{1,2,0:T(8,128)(2,1)} %param.18) | copy-start | bytes 737284
  7.2 20.8 %copy-start.35 = (bf16[240,320]{0,1:T(8,128)(2,1)S(1)}, bf16[240,320]{0,1:T(8,128)(2,1)}, u32[]{:S(2)}) copy-start(bf16[240,320]{0,1:T(8,128)(2,1)} %param.21) | copy-start | bytes 460804
  7.2 40.1 %all-gather.13.cloned.1.call-start = ((), (), s32[]{:S(2)}) async-start(), calls=%async_computation.10 | async-start | bytes 2457600 | tf_op jit(solution)/shard_map/all_gather | solution.py:211
  8.0 123.0 %all-gather.23.cloned.1.call-start = ((), (), s32[]{:S(2)}) async-start(), calls=%async_computation.17 | async-start | bytes 2703360 | tf_op jit(solution)/shard_map/all_gather | solution.py:253
  17.7 21.8 %copy-start.22 = (bf16[960,320]{0,1:T(8,128)(2,1)}, bf16[960,320]{0,1:T(8,128)(2,1)S(1)}, u32[]{:S(2)}) copy-start(bf16[960,320]{0,1:T(8,128)(2,1)S(1)} %reshape.454) | copy-start | bytes 1843204
  17.7 22.9 %copy-start.37 = (s32[1,32]{1,0:T(1,128)S(1)}, s32[1,32]{1,0:T(1,128)}, u32[]{:S(2)}) copy-start(s32[1,32]{1,0:T(1,128)} %param.19) | copy-start | bytes 388
  27.9 187.6 %all-gather.11.cloned.1.call-start = ((), (), s32[]{:S(2)}) async-start(), calls=%async_computation.9 | async-start | bytes 2703360 | tf_op jit(solution)/shard_map/all_gather | solution.py:247
  40.6 6.1 copy-start.15
  44.2 252.9 %all-gather.15.cloned.1.call-start = ((), (), s32[]{:S(2)}) async-start(), calls=%async_computation.11 | async-start | bytes 2457600 | tf_op jit(solution)/shard_map/all_gather | solution.py:214
  44.8 255.9 %all-gather.17.cloned.1.call-start = ((), (), s32[]{:S(2)}) async-start(), calls=%async_computation.12 | async-start | bytes 6144000 | tf_op jit(solution)/shard_map/all_gather | solution.py:282
  45.4 307.8 %all-gather.19.cloned.1.call-start = ((), (), s32[]{:S(2)}) async-start(), calls=%async_computation.13 | async-start | bytes 6144000 | tf_op jit(solution)/shard_map/all_gather | solution.py:283
  46.0 362.4 %all-gather.21.cloned.1.call-start = ((), (), s32[]{:S(2)}) async-start(), calls=%async_computation.14 | async-start | bytes 6144000 | tf_op jit(solution)/shard_map/all_gather | solution.py:284
  46.7 722.5 %reduce-scatter.28.cloned.1.call-start = ((), (), s32[]{:S(2)}) async-start(), calls=%async_computation.18 | async-start | bytes 3244032
  413.9 4.4 copy-start.9
  541.5 456.5 %reduce-scatter.30.cloned.1.call-start = ((), (), s32[]{:S(2)}) async-start(), calls=%async_computation.19 | async-start | bytes 3244032
  567.4 475.8 %reduce-scatter.32.cloned.1.call-start = ((), (), s32[]{:S(2)}) async-start(), calls=%async_computation.20 | async-start | bytes 921600
  770.9 230.0 %copy-start.19 = (bf16[128,2560]{1,0:T(8,128)(2,1)S(1)}, bf16[128,2560]{1,0:T(8,128)(2,1)}, u32[]{:S(2)}) copy-start(bf16[128,2560]{1,0:T(8,128)(2,1)} %copy-done.18) | copy-start | bytes 1966084
  772.1 272.7 %reduce-scatter.34.cloned.1.call-start = ((), (), s32[]{:S(2)}) async-start(), calls=%async_computation.21 | async-start | bytes 921600
  1000.9 96.5 %reduce-scatter.36.cloned.1.call-start = ((), (), s32[]{:S(2)}) async-start(), calls=%async_computation.22 | async-start | bytes 6553600
  1012.4 142.4 %reduce-scatter.38.cloned.1.call-start = ((), (), s32[]{:S(2)}) async-start(), calls=%async_computation.23 | async-start | bytes 6553600
  1025.0 187.0 %reduce-scatter.40.cloned.1.call-start = ((), (), s32[]{:S(2)}) async-start(), calls=%async_computation.24 | async-start | bytes 6553600
  1037.6 205.4 %reduce-scatter.24.cloned.1.call-start = ((), (), s32[]{:S(2)}) async-start(), calls=%async_computation.15 | async-start | bytes 2457600 | tf_op jit(solution)/shard_map/reduce_scatter | solution.py:383
  1040.8 233.3 %reduce-scatter.26.cloned.1.call-start = ((), (), s32[]{:S(2)}) async-start(), calls=%async_computation.16 | async-start | bytes 2457600 | tf_op jit(solution)/shard_map/reduce_scatter | solution.py:392
  1042.9 608.6 %all-reduce.10.cloned.1.call-start = ((), (), s32[]{:S(2)}) async-start(), calls=%async_computation.25 | async-start | bytes 9994240 | tf_op jit(solution)/shard_map/psum | solution.py:412
  1214.4 60.4 %copy-start.10 = (f32[128,960]{0,1:T(8,128)S(1)}, f32[128,960]{0,1:T(8,128)}, u32[]{:S(2)}) copy-start(f32[128,960]{0,1:T(8,128)} %copy-done.8) | copy-start | bytes 1474564
  1274.8 4.7 copy-start.23
  1274.8 5.1 copy-start.16
  1651.5 5.5 copy-start.34
  1651.5 6.6 copy-start.31
  (67 other events, 168.0 us)
Sparse Core Ops, SparseCore 0:
  9.7 34.0 all-gather.12
  47.1 83.7 all-gather.22
  134.3 81.1 all-gather.10
  217.0 26.6 all-gather.14
  245.2 52.8 all-gather.16
  299.7 53.4 all-gather.18
  354.9 53.4 all-gather.20
  541.6 227.5 reduce-scatter.27
  774.9 223.0 reduce-scatter.29
  1000.9 16.2 reduce-scatter.31
  1020.1 19.8 reduce-scatter.33
  1042.3 54.9 reduce-scatter.35
  1099.8 54.9 reduce-scatter.37
  1157.0 54.9 reduce-scatter.39
  1214.8 28.1 reduce-scatter.23
  1245.9 28.1 reduce-scatter.25
  1278.2 373.2 all-reduce.9
where the time goes:
time: 1680 us; the launch traced here: 1670 us
  waiting for transfers between devices  1170 us (70%)
  matrix products  185 us (11%)
  blocking collectives  129 us (8%)
  local copies, waits for them, and re-layouts  114 us (7%)
  other arithmetic  47.3 us (3%)
    unnamed x24, waiting for transfers between devices  591 us
    psum x1, waiting for transfers between devices, body(): lax.psum(shard_query.astype(jnp.bfloat16), 'ctx').astype(jnp.float32)  265 us
    psum x1, blocking collectives, body(): lax.psum(shard_gain_one.astype(jnp.bfloat16), 'ctx').astype(jnp.float32)  96.5 us
    unnamed x99, local copies, waits for them, and re-layouts  94.5 us
    all_gather x1, waiting for transfers between devices, body(): lax.all_gather(resident_value.reshape(sequence_count, resident_rows, KEY_...  79.9 us
    all_gather x1, waiting for transfers between devices, body(): lax.all_gather(resident_key.reshape(sequence_count, resident_rows, KEY_VA...  79.3 us
    all_gather x1, waiting for transfers between devices, body(): lax.all_gather(w_down, 'fsdp', axis=0, tiled=True)  50.9 us
    all_gather x1, waiting for transfers between devices, body(): lax.all_gather(w_up, 'fsdp', axis=1, tiled=True)  48.2 us
  transfers between devices with their start and end apart: 17, of which 12 were waited for; matrix products, arithmetic and copies ran while one was open for 12% of the time, Pallas kernels for 0%

commit v1 on v0

v1 whole, which is shorter than its diff:
```python
import jax
import jax.numpy as jnp
from jax import lax
from jax.sharding import Mesh, PartitionSpec as P

QUERY_HEADS = 15
KEY_VALUE_HEADS = 5
HEAD_SIZE = 64
EPSILON = 1e-05
BF = jnp.bfloat16
F32 = jnp.float32
FS = ("zl", "co")
RING = (0, -1, 1, 2)


def matrix_product(left, right):
    return jnp.dot(left, right, preferred_element_type=F32)


def left_inner(left, right):
    return lax.dot_general(left, right, (((0,), (0,)), ((), ())), preferred_element_type=F32)


def right_inner(left, right):
    return lax.dot_general(left, right, (((1,), (1,)), ((), ())), preferred_element_type=F32)


def shift(value, axis, step):
    count = lax.axis_size(axis)
    return lax.ppermute(value, axis, [(i, (i + step) % count) for i in range(count)])


def ring_gather(value, axis):
    half = value.shape[0] // 2
    left = shift(value, axis, 1)
    right = shift(value, axis, -1)
    far_one = shift(left[:half], axis, 1)
    far_two = shift(right[half:], axis, -1)
    return jnp.concatenate([value, left, right, far_one, far_two], axis=0)


def add_low(*parts):
    total = parts[0].astype(F32)
    for part in parts[1:]:
        total = total + part.astype(F32)
    return total.astype(BF)


def ring_scatter(value, axis):
    rows = value.shape[0] // 4
    half = rows // 2
    own, left, right = value[:rows], value[rows : 2 * rows], value[2 * rows : 3 * rows]
    from_left = shift(value[3 * rows : 3 * rows + half], axis, 1)
    from_right = shift(value[3 * rows + half :], axis, -1)
    right = jnp.concatenate([add_low(right[:half], from_left), right[half:]], axis=0)
    left = jnp.concatenate([left[:half], add_low(left[half:], from_right)], axis=0)
    return add_low(own, shift(right, axis, 1), shift(left, axis, -1))


def ring_pick(value, axis):
    here = lax.axis_index(axis)
    return jnp.concatenate(
        [lax.dynamic_slice_in_dim(value, lax.rem(here + off + 4, 4), 1, axis=0) for off in RING], axis=0
    )


def ring_place(value, axis):
    here = lax.axis_index(axis)
    out = value
    for place, off in enumerate(RING):
        out = lax.dynamic_update_slice_in_dim(
            out, value[place : place + 1], lax.rem(here + off + 4, 4), axis=0
        )
    return out


def pair_gather(value):
    both = jnp.concatenate([value[None], shift(value, "zl", 1)[None]], axis=0)
    other = shift(both, "co", 1)
    return jnp.stack([both[0], other[0], both[1], other[1]])


def pair_scatter(value):
    near = add_low(value[:2], shift(value[2:].astype(BF), "zl", 1))
    return near[0].astype(F32) + shift(near[1], "co", 1).astype(F32)


def weight_gather(value):
    rows = value.shape[0]
    cut = 128
    zed = ("zh", "zl")
    one = shift(value[:cut], zed, 1)
    two = shift(value[cut:], zed, -1)
    core = shift(value, "co", 1)
    core_one = shift(one, "co", 1)
    core_two = shift(two, "co", 1)
    place = 2 * lax.axis_index("zl") + lax.axis_index("co")
    out = jnp.zeros((4, rows) + value.shape[1:], value.dtype)
    for mask, block in (
        (0, value),
        (1, core),
        (2, jnp.concatenate([one, two], axis=0)),
        (3, jnp.concatenate([core_one, core_two], axis=0)),
    ):
        out = lax.dynamic_update_slice_in_dim(out, block[None], place ^ mask, axis=0)
    return out.reshape((4 * rows,) + value.shape[1:])


def direct_scatter(value, axis):
    near = [shift(value[place], axis, off) for place, off in ((1, -1), (2, 1), (3, 2))]
    return add_low(value[0], *near)


def direct_gather(value, axis):
    return jnp.stack([value, shift(value, axis, 1), shift(value, axis, -1), shift(value, axis, 2)])


def wide_gather(value, axis):
    left = shift(value, axis, 1)
    right = shift(value, axis, -1)
    far_one = shift(left[:, :2], axis, 1)
    far_two = shift(right[:, 2:], axis, -1)
    return jnp.concatenate([value, left, right, jnp.concatenate([far_one, far_two], axis=1)], axis=0)


def wide_scatter(value, axis):
    own, left, right = value[0], value[1], value[2]
    half = own.shape[0] // 2
    from_left = shift(value[3, :half], axis, 1)
    from_right = shift(value[3, half:], axis, -1)
    right = jnp.concatenate([add_low(right[:half], from_left), right[half:]], axis=0)
    left = jnp.concatenate([left[:half], add_low(left[half:], from_right)], axis=0)
    return add_low(own, shift(right, axis, 1), shift(left, axis, -1))


def reduce_sum(value, first, second):
    shape = value.shape
    out = value.reshape((4, 4) + shape[1:])
    out = wide_scatter(ring_pick(out, first), first)
    out = direct_scatter(ring_pick(out, second), second)
    out = add_low(out, shift(out, "zh", 1))
    out = ring_place(direct_gather(out, second), second)[None]
    out = ring_place(wide_gather(out, first), first)
    return out.reshape(shape)


def context_gather(value, first, second):
    out = jnp.stack([value, shift(value, "zh", 1)])
    return ring_gather(ring_gather(out, first), second)


def context_scatter(value, first, second):
    out = ring_scatter(ring_scatter(value, second), first)
    return out[0].astype(F32) + shift(out[1], "zh", 1).astype(F32)


def swap_order(value):
    return jnp.swapaxes(value.reshape((4, 4, 2) + value.shape[1:]), 0, 1).reshape(value.shape)


def apply_rotation(values, cosine_table, sinusoid_table):
    half = values.shape[-1] // 2
    leading, trailing = values[..., :half], values[..., half:]
    return jnp.concatenate(
        [
            leading * cosine_table - trailing * sinusoid_table,
            trailing * cosine_table + leading * sinusoid_table,
        ],
        axis=-1,
    )


def norm_forward(values, gain_vector):
    inverse = lax.rsqrt(jnp.mean(values * values, axis=-1, keepdims=True) + EPSILON)
    return (values * inverse * gain_vector, inverse)


def norm_backward(values, inverse, gain_vector, gradient):
    weighted = gradient * gain_vector
    through = inverse * weighted - values * inverse**3 * jnp.mean(
        weighted * values, axis=-1, keepdims=True
    )
    return (through, jnp.sum(gradient * values * inverse, axis=0))


def pair_positions(pair_rows, count, span):
    block_list = jnp.stack([pair_rows, 2 * count - 1 - pair_rows], axis=-1)
    offsets = jnp.arange(span, dtype=jnp.int32)
    return (block_list[..., None] * span + offsets).reshape(-1)


def masked_scores(query_rows, key_block, query_places, key_places, factor):
    scores = (
        jnp.einsum("qkgd,skd->kgqs", query_rows, key_block, preferred_element_type=F32) * factor
    )
    allowed = query_places[:, None] >= key_places[None, :]
    return jnp.where(allowed[None, None], scores, -1e30)


def split_blocks(rows_of_key, rows_of_value, key_places):
    return (
        rows_of_key.reshape((8, 512) + rows_of_key.shape[1:]),
        rows_of_value.reshape((8, 512) + rows_of_value.shape[1:]),
        key_places.reshape(8, 512),
    )


def attention_forward(query_rows, rows_of_key, rows_of_value, query_places, key_places, factor):
    blocks = split_blocks(rows_of_key, rows_of_value, key_places)
    shape_stat = (query_rows.shape[1], query_rows.shape[2], query_rows.shape[0])

    def statistics(running, block_item):
        running_max, running_sum = running
        key_block, _, key_place = block_item
        scores = masked_scores(query_rows, key_block, query_places, key_place, factor)
        new_max = jnp.maximum(running_max, jnp.max(scores, axis=-1))
        running_sum = running_sum * jnp.exp(running_max - new_max) + jnp.sum(
            jnp.exp(scores - new_max[..., None]), axis=-1
        )
        return ((new_max, running_sum), None)

    (row_max, row_sum), _ = lax.scan(
        statistics, (jnp.full(shape_stat, -1e30, F32), jnp.zeros(shape_stat, F32)), blocks
    )
    log_total = row_max + jnp.log(row_sum)

    def accumulate(running, block_item):
        key_block, value_block, key_place = block_item
        scores = masked_scores(query_rows, key_block, query_places, key_place, factor)
        soft_weights = jnp.exp(scores - log_total[..., None]).astype(BF)
        return (
            running
            + jnp.einsum("kgqs,skd->qkgd", soft_weights, value_block, preferred_element_type=F32),
            None,
        )

    attended, _ = lax.scan(accumulate, jnp.zeros(query_rows.shape, F32), blocks)
    return (attended, log_total)


def attention_backward(
    query_rows, rows_of_key, rows_of_value, query_places, key_places, factor, attended, log_total, attended_gradient
):
    blocks = split_blocks(rows_of_key, rows_of_value, key_places)
    row_delta = jnp.transpose(
        jnp.sum(attended_gradient.astype(F32) * attended, axis=-1), (1, 2, 0)
    )

    def backward_block(running, block_item):
        key_block, value_block, key_place = block_item
        scores = masked_scores(query_rows, key_block, query_places, key_place, factor)
        soft_weights = jnp.exp(scores - log_total[..., None])
        grad_soft = jnp.einsum(
            "qkgd,skd->kgqs", attended_gradient, value_block, preferred_element_type=F32
        )
        grad_scores = (soft_weights * (grad_soft - row_delta[..., None])).astype(BF)
        running = running + jnp.einsum(
            "kgqs,skd->qkgd", grad_scores, key_block, preferred_element_type=F32
        )
        grad_key_block = (
            jnp.einsum("kgqs,qkgd->skd", grad_scores, query_rows, preferred_element_type=F32) * factor
        ).astype(BF)
        grad_value_block = jnp.einsum(
            "kgqs,qkgd->skd", soft_weights.astype(BF), attended_gradient, preferred_element_type=F32
        ).astype(BF)
        return (running, (grad_key_block, grad_value_block))

    grad_queries, (grad_key_rows, grad_value_rows) = lax.scan(
        backward_block, jnp.zeros(query_rows.shape, F32), blocks
    )
    return (grad_queries * factor, grad_key_rows, grad_value_rows)


def body(
    tokens, block_pairs, w_query, key_weight, value_weight, w_out, gain_attn, gain_mlp, w_gate, w_up, w_down, cotangent
):
    rows, width = tokens.shape[1:]
    kv_width = KEY_VALUE_HEADS * HEAD_SIZE
    factor = HEAD_SIZE ** (-0.5)
    x_here, y_here, z_here = lax.axis_index("x"), lax.axis_index("y"), lax.axis_index("zh")
    place = 2 * lax.axis_index("zl") + lax.axis_index("co")
    context = z_here * 16 + x_here * 4 + y_here

    weights_in = weight_gather(jnp.concatenate([w_query, key_weight, value_weight], axis=1))
    out_w = weight_gather(w_out)
    gains = lax.all_gather(jnp.stack([gain_attn, gain_mlp])[None], FS, axis=0, tiled=True)
    gains = jnp.swapaxes(gains, 0, 1).reshape(2, width).astype(F32)
    gain_one, gain_two = gains[0], gains[1]

    inputs = tokens[0].astype(F32)
    upstream = cotangent[0].astype(F32)
    grad_mlp = pair_gather(cotangent[0]).reshape(4 * rows, width)

    order = [
        ((z_here + z) % 2) * 16 + ((x_here + x + 4) % 4) * 4 + (y_here + y + 4) % 4
        for x in RING
        for y in RING
        for z in (0, 1)
    ]
    pairs = block_pairs[0][jnp.stack(order)]
    query_places = pair_positions(pairs[:1], 32, rows // 2)
    key_places = pair_positions(pairs, 32, rows // 2)
    frequency = 10000.0 ** (-jnp.arange(HEAD_SIZE // 2, dtype=F32) / (HEAD_SIZE // 2))
    angles = query_places.astype(F32)[:, None] * frequency[None, :]
    cosine_table, sinusoid_table = jnp.cos(angles)[:, None, :], jnp.sin(angles)[:, None, :]

    normed_one, inverse_one = norm_forward(inputs, gain_one)
    normed_low = normed_one.astype(BF)
    projected = matrix_product(normed_low, weights_in)
    heads = QUERY_HEADS + KEY_VALUE_HEADS
    rotated = apply_rotation(
        projected[:, : width + kv_width].reshape(rows, heads, HEAD_SIZE), cosine_table, sinusoid_table
    ).astype(BF)
    queries = rotated[:, :QUERY_HEADS]
    keys = rotated[:, QUERY_HEADS:].reshape(rows, kv_width)
    values = projected[:, width + kv_width :].astype(BF)

    all_keys = context_gather(keys, "y", "x")
    all_values = swap_order(context_gather(values, "x", "y"))
    grouped = queries.reshape(rows, KEY_VALUE_HEADS, -1, HEAD_SIZE)
    heads_of_key = all_keys.reshape(-1, KEY_VALUE_HEADS, HEAD_SIZE)
    heads_of_value = all_values.reshape(-1, KEY_VALUE_HEADS, HEAD_SIZE)
    attended, log_total = attention_forward(
        grouped, heads_of_key, heads_of_value, query_places, key_places, factor
    )
    attended_low = attended.reshape(rows, width).astype(BF)
    middle = inputs + matrix_product(attended_low, out_w)
    normed_two, inverse_two = norm_forward(middle, gain_two)
    normed_mlp = pair_gather(normed_two.astype(BF)).reshape(4 * rows, width)

    gate_pre = matrix_product(normed_mlp, w_gate)
    up_pre = matrix_product(normed_mlp, w_up)
    grad_hidden = right_inner(grad_mlp, w_down)
    sigmoid_gate = jax.nn.sigmoid(gate_pre)
    hidden = (gate_pre * sigmoid_gate * up_pre).astype(BF)
    grad_up_pre = (grad_hidden * gate_pre * sigmoid_gate).astype(BF)
    grad_gate_pre = (
        grad_hidden * up_pre * sigmoid_gate * (1.0 + gate_pre * (1.0 - sigmoid_gate))
    ).astype(BF)
    grad_normed_two = right_inner(grad_gate_pre, w_gate) + right_inner(grad_up_pre, w_up)
    grad_normed_two = pair_scatter(grad_normed_two.astype(BF).reshape(4, rows, width))
    mlp_term = pair_scatter(matrix_product(hidden, w_down).astype(BF).reshape(4, rows, width))
    result = (middle + mlp_term).astype(BF)[None]

    pad = ((0, 64), (0, 0))
    grad_gate_w = jnp.pad(left_inner(normed_mlp, grad_gate_pre).astype(BF), pad).reshape(16, 64, -1)
    grad_up_w = jnp.pad(left_inner(normed_mlp, grad_up_pre).astype(BF), pad).reshape(16, 64, -1)
    grad_down_w = jnp.pad(left_inner(grad_mlp, hidden).astype(BF), pad).reshape(2, 16, 32, -1)
    sum_one = reduce_sum(jnp.concatenate([grad_gate_w, grad_down_w[0]], axis=1), "x", "y")
    sum_two = reduce_sum(jnp.concatenate([grad_up_w, grad_down_w[1]], axis=1), "y", "x")

    through_two, grad_gain_two = norm_backward(middle, inverse_two, gain_two, grad_normed_two)
    grad_middle = upstream + through_two
    grad_branch = grad_middle.astype(BF)
    attended_gradient = right_inner(grad_branch, out_w).astype(BF)
    grad_queries, key_gradients, value_gradients = attention_backward(
        grouped,
        heads_of_key,
        heads_of_value,
        query_places,
        key_places,
        factor,
        attended,
        log_total,
        attended_gradient.reshape(grouped.shape),
    )
    own_key_gradient = context_scatter(key_gradients.reshape(32, rows, kv_width), "y", "x")
    own_value_gradient = context_scatter(
        swap_order(value_gradients.reshape(32, rows, kv_width)), "x", "y"
    )
    grad_query_pre = (
        apply_rotation(grad_queries.reshape(rows, QUERY_HEADS, HEAD_SIZE), cosine_table, -sinusoid_table)
        .reshape(rows, width)
        .astype(BF)
    )
    grad_key_pre = (
        apply_rotation(
            own_key_gradient.reshape(rows, KEY_VALUE_HEADS, HEAD_SIZE), cosine_table, -sinusoid_table
        )
        .reshape(rows, kv_width)
        .astype(BF)
    )
    grad_kv = jnp.concatenate([grad_key_pre, own_value_gradient.astype(BF)], axis=1)

    def own_columns(value):
        blocks = value.T.reshape(4, width // 4, rows)
        parts = []
        for mask in range(4):
            part = lax.dynamic_index_in_dim(blocks, place ^ mask, axis=0, keepdims=False)
            if mask:
                part = lax.ppermute(part, FS, [(i, i ^ mask) for i in range(4)])
            parts.append(part)
        return jnp.concatenate(parts, axis=1)

    normed_columns = own_columns(normed_low)
    attended_columns = own_columns(attended_low)
    all_branch = pair_gather(grad_branch).reshape(4 * rows, width)
    all_query = pair_gather(grad_query_pre).reshape(4 * rows, width)
    all_kv = pair_gather(grad_kv).reshape(4 * rows, 2 * kv_width)
    pad = ((0, 16), (0, 0))
    grad_out_w = jnp.pad(matrix_product(attended_columns, all_branch).astype(BF), pad)
    grad_query_w = jnp.pad(matrix_product(normed_columns, all_query).astype(BF), pad)
    sum_out = reduce_sum(grad_out_w.reshape(16, 16, width), "x", "y")
    sum_query = reduce_sum(grad_query_w.reshape(16, 16, width), "y", "x")

    grad_kv_w = matrix_product(normed_columns, all_kv).astype(BF)
    grad_normed_one = right_inner(jnp.concatenate([grad_query_pre, grad_kv], axis=1), weights_in)
    through_one, grad_gain_one = norm_backward(inputs, inverse_one, gain_one, grad_normed_one)
    input_grad = (grad_middle + through_one)[None]

    grad_gains = jnp.stack([grad_gain_one, grad_gain_two]).astype(BF)
    grad_gains = lax.psum(grad_gains, FS)
    grad_gains = lax.dynamic_slice_in_dim(grad_gains, place * (width // 4), width // 4, axis=1)
    last = jnp.concatenate(
        [grad_kv_w, jnp.pad(grad_gains, ((0, 14), (0, 2 * kv_width - width // 4)))], axis=0
    )
    sum_last = reduce_sum(last.reshape(16, 16, 2 * kv_width), "x", "y").reshape(256, 2 * kv_width)

    quarter = width // 4
    hidden_shard = w_gate.shape[1]
    sum_down = jnp.concatenate(
        [sum_one[:, 64:].reshape(512, hidden_shard), sum_two[:, 64:].reshape(512, hidden_shard)], axis=0
    )[:width]
    return (
        result,
        input_grad,
        sum_query.reshape(256, width)[:quarter].astype(F32),
        sum_last[:quarter, :kv_width].astype(F32),
        sum_last[:quarter, kv_width:].astype(F32),
        sum_out.reshape(256, width)[:quarter].astype(F32),
        sum_last[quarter, :quarter].astype(F32),
        sum_last[quarter + 1, :quarter].astype(F32),
        sum_one[:, :64].reshape(1024, hidden_shard)[:width].astype(F32),
        sum_two[:, :64].reshape(1024, hidden_shard)[:width].astype(F32),
        sum_down.T.astype(F32),
    )


def solution(mesh):
    split = Mesh(mesh.devices.reshape(2, 4, 4, 2, 2), ("zh", "x", "y", "zl", "co"))
    ctx = ("zh", "x", "y")
    in_specs = (
        P(FS, ctx, None),
        P(FS, None),
        P(FS, None),
        P(FS, None),
        P(FS, None),
        P(FS, None),
        P(FS),
        P(FS),
        P(None, FS),
        P(None, FS),
        P(FS, None),
        P(FS, ctx, None),
    )
    out_specs = (
        P(FS, ctx, None),
        P(FS, ctx, None),
        P(FS, None),
        P(FS, None),
        P(FS, None),
        P(FS, None),
        P(FS),
        P(FS),
        P(None, FS),
        P(None, FS),
        P(FS, None),
    )
    return jax.shard_map(body, mesh=split, in_specs=in_specs, out_specs=out_specs, check_vma=False)
```

time: 1680 us -> 740 us (0.44)
  waiting for transfers between devices: 1170 us -> 145 us
  starting transfers between devices: 1.03 us -> 193 us
  blocking collectives: 129 us -> 11.6 us
  other arithmetic: 47.3 us -> 67 us
    unnamed x24 -> x0, waiting for transfers between devices: 591 us -> none
    psum x1 -> x0, waiting for transfers between devices: 265 us -> none  [body(): lax.psum(shard_query.astype(jnp.bfloat16), 'ctx').astype(jnp.float32)]
    all_gather x7 -> x0, waiting for transfers between devices: 258 us -> none  [the longest x1 79.9 us: body(): lax.all_gather(resident_value.reshape(sequence_count, resident_rows, KEY_...]
    ppermute x0 -> x141, starting transfers between devices: none -> 193 us  [the longest x135 189 us: shift(): lax.ppermute(value, axis, [(i, (i + step) % count) for i in range(count)])]
    ppermute x0 -> x141, waiting for transfers between devices: none -> 145 us  [the longest x135 142 us: shift(): lax.ppermute(value, axis, [(i, (i + step) % count) for i in range(count)])]
    psum x1, blocking collectives: 96.5 us -> 5.68 us  [body(): grad_gains = lax.psum(grad_gains, FS)]
    reduce_scatter x2 -> x0, waiting for transfers between devices: 59.7 us -> none  [the longest x1 31.1 us: body(): lax.psum_scatter(grad_out_w.astype(jnp.bfloat16), 'fsdp', scatter_dimensi...]
    unnamed x99 -> x156, local copies, waits for them, and re-layouts: 94.5 us -> 35.4 us
  transfers between devices with their start and end apart: 17 -> 141, of which waited for: 12 -> 59; matrix products, arithmetic and copies ran while one was open for 12% -> 49% of each run, Pallas kernels for 0% -> 0%
where the time goes in v1:
time: 740 us; the launch traced here: 728 us
  starting transfers between devices  193 us (26%)
  matrix products  180 us (24%)
  waiting for transfers between devices  145 us (20%)
  local copies, waits for them, and re-layouts  127 us (17%)
  other arithmetic  67 us (9%)
  blocking collectives  11.6 us (2%)
    ppermute x135, starting transfers between devices, shift(): lax.ppermute(value, axis, [(i, (i + step) % count) for i in range(count)])  189 us
    ppermute x135, waiting for transfers between devices, shift(): lax.ppermute(value, axis, [(i, (i + step) % count) for i in range(count)])  142 us
    dot_general x16, matrix products, masked_scores(): jnp.einsum('qkgd,skd->kgqs', query_rows, key_block, preferred_element_typ...  58.7 us
    unnamed x156, local copies, waits for them, and re-layouts  35.4 us
    dot_general x8, matrix products, backward_block(): jnp.einsum('qkgd,skd->kgqs', attended_gradient, value_block, preferred_el...  29.1 us
    reduce_sum x8, other arithmetic, statistics(): jnp.sum(jnp.exp(scores - new_max[..., None]), axis=-1)  23.4 us
    dot_general x8, matrix products, backward_block(): jnp.einsum('kgqs,qkgd->skd', soft_weights.astype(BF), attended_gradient,...  22.6 us
    dot_general x8, matrix products, accumulate(): jnp.einsum('kgqs,skd->qkgd', soft_weights, value_block, preferred_element...  19.9 us
  transfers between devices with their start and end apart: 141, of which 59 were waited for; matrix products, arithmetic and copies ran while one was open for 49% of the time, Pallas kernels for 0%

profile of v1, /device:TPU:0, one launch (start us, length us, event | category | flops | bytes accessed | tf_op | source)
XLA Modules:
  0.0 727.8 jit_solution(16105282131696312806)
XLA Ops:
  6.8 4.1 collective-permute-start.2
  18.3 5.9 all-gather.1
  43.1 3.7 collective-permute-start.5
  48.4 5.2 collective-permute-done.14
  112.3 5.0 copy.168
  117.4 5.3 reshape_reshape.27
  122.7 4.2 copy.171
  126.9 55.5 %while.39 = (s32[]{:T(128)}, f32[5,3,128]{2,1,0:T(4,128)S(1)}, f32[5,3,128]{2,1,0:T(4,128)S(1)}, s32[8,512]{1,0:T(8,128)S(1)}, bf16[8,512,5,64]{1,3,2,0:T(8,128)...) while((s32[]{:T(128)}, f32[5,3,128]{2,1,0:T(4,128)S(1)}, ...), condition=%wide.region_4.5_spmd.clone, body=%wide.region_1.4_spmd.clone.sunk | while | flops 132785664 | bytes 8742528 | solution.py:222
  185.8 5.9 copy.266
  191.7 5.1 reshape_reshape_reshape.4
  196.9 4.2 copy.170
  201.1 22.6 %while.40 = (s32[]{:T(128)}, f32[128,5,3,64]{0,3,2,1:T(8,128)S(1)}, bf16[8,512,5,64]{1,3,2,0:T(8,128)(2,1)}, s32[8,512]{1,0:T(8,128)S(1)}, bf16[8,512,5,64]{1,3,...) while((s32[]{:T(128)}, f32[128,5,3,64]{0,3,2,1:T(8,128)S(1)}, ...), condition=%wide.region_6.7_spmd.clone, body=%wide.region_5.6_spmd.clone.sunk | while | flops 255901824 | bytes 2032770 | solution.py:237
  226.4 9.9 %collective-permute-start.28 = (bf16[128,960]{0,1:T(8,128)(2,1)S(1)}, bf16[128,960]{0,1:T(8,128)(2,1)S(1)}, u32[]{:S(2)}, u32[]{:S(2)}) collective-permute-start(bf16[128,960]{0,1:T(8,128)(2,1)S(1)} %multiply_convert_fusion.3), channel_id=1, source_target_pairs={{0,2},{2,0},{1,3},{3,1},{4,6},{6,4},{5,7},{7,5},{8,10},{10,8},{9,1... | collective-permute-start | bytes 737288 | tf_op jit(solution)/shard_map/ppermute | solution.py:30
  265.1 3.9 collective-permute-done.128
  286.8 109.3 %while.41 = (s32[]{:T(128)}, f32[128,5,3,64]{0,3,2,1:T(8,128)S(1)}, bf16[8,512,5,64]{1,3,2,0:T(8,128)(2,1)}, bf16[8,512,5,64]{1,3,2,0:T(8,128)(2,1)}, bf16[8,512...) while((s32[]{:T(128)}, f32[128,5,3,64]{0,3,2,1:T(8,128)S(1)}, ...), condition=%wide.region_11.12_spmd.clone, body=%wide.region_10.11_spmd.clone.sunk | while | flops 639778944 | bytes 39222024 | solution.py:268
  300.5 3.7 fusion.276
  341.5 3.7 fusion.276
  355.2 3.7 fusion.276
  382.5 3.7 fusion.276
  396.1 4.7 copy.188
  400.8 4.9 reshape_reshape.28
  456.6 3.7 collective-permute-start.133
  513.6 12.8 %collective-permute-done.97 = bf16[4,16,960]{2,1,0:T(8,128)(2,1)S(1)} collective-permute-done((bf16[4,16,960]{2,1,0:T(8,128)(2,1)S(1)}, bf16[4,16,960]{2,1,0:T(8,128)(2,1)S(1)}, u32[]{:S(2)}, u32[]{:S(2)}) %collective-permute-start.97) | collective-permute-done | bytes 122912 | tf_op jit(solution)/shard_map/ppermute | solution.py:30
  531.7 6.1 collective-permute-done.123
  538.3 3.7 collective-permute-done.102
  591.8 3.8 collective-permute-done.109
  595.6 4.3 collective-permute-done.110
  600.0 6.4 collective-permute-done.41
  639.8 3.7 collective-permute-done.60
  651.2 4.0 collective-permute-done.66
  667.9 5.7 psum.7
  698.6 4.6 collective-permute-done.83
  (944 shorter events, 577.6 us)
Async XLA Ops:
  5.0 28.6 %collective-permute-start = (bf16[240,1600]{1,0:T(8,128)(2,1)}, bf16[240,1600]{1,0:T(8,128)(2,1)}, u32[]{:S(2)}, u32[]{:S(2)}) collective-permute-start(bf16[240,1600]{1,0:T(8,128)(2,1)} %concatenate.199), channel_id=1, source_target_pairs={{0,1},{1,0},{2,3},{3,2},{4,5},{5,4},{6,7},{7,6},{8,9},{9,8},{10,11... | collective-permute-start | bytes 2304008 | tf_op jit(solution)/shard_map/ppermute | solution.py:30
  6.8 26.2 %collective-permute-start.2 = (bf16[112,1600]{1,0:T(8,128)(2,1)}, bf16[112,1600]{1,0:T(8,128)(2,1)}, u32[]{:S(2)}, u32[]{:S(2)}) collective-permute-start(bf16[112,1600]{1,0:T(8,128)(2,1)} %slice.646), channel_id=1, source_target_pairs={{0,66},{2,0},{64,2},{66,64},{1,67},{3,1},{65,3},{67,65},{4,70},{6,... | collective-permute-start | bytes 1075208 | tf_op jit(solution)/shard_map/ppermute | solution.py:30
  12.7 20.7 %collective-permute-start.1 = (bf16[128,1600]{1,0:T(8,128)(2,1)}, bf16[128,1600]{1,0:T(8,128)(2,1)}, u32[]{:S(2)}, u32[]{:S(2)}) collective-permute-start(bf16[128,1600]{1,0:T(8,128)(2,1)} %slice.645), channel_id=1, source_target_pairs={{0,2},{2,64},{64,66},{66,0},{1,3},{3,65},{65,67},{67,1},{4,6},{6,6... | collective-permute-start | bytes 1228808 | tf_op jit(solution)/shard_map/ppermute | solution.py:30
  14.3 47.3 %collective-permute-start.25 = (bf16[112,960]{1,0:T(8,128)(2,1)}, bf16[112,960]{1,0:T(8,128)(2,1)}, u32[]{:S(2)}, u32[]{:S(2)}) collective-permute-start(bf16[112,960]{1,0:T(8,128)(2,1)} %slice.515), channel_id=1, source_target_pairs={{0,66},{2,0},{64,2},{66,64},{1,67},{3,1},{65,3},{67,65},{4,70},{6,... | collective-permute-start | bytes 645128 | tf_op jit(solution)/shard_map/ppermute | solution.py:30
  61.6 23.7 %collective-permute-start.23 = (bf16[240,960]{1,0:T(8,128)(2,1)}, bf16[240,960]{1,0:T(8,128)(2,1)}, u32[]{:S(2)}, u32[]{:S(2)}) collective-permute-start(bf16[240,960]{1,0:T(8,128)(2,1)} %param.23), channel_id=1, source_target_pairs={{0,1},{1,0},{2,3},{3,2},{4,5},{5,4},{6,7},{7,6},{8,9},{9,8},{10,11... | collective-permute-start | bytes 1382408 | tf_op jit(solution)/shard_map/ppermute | solution.py:30
  61.7 18.7 %collective-permute-start.27 = (bf16[112,960]{1,0:T(8,128)(2,1)}, bf16[112,960]{1,0:T(8,128)(2,1)S(1)}, u32[]{:S(2)}, u32[]{:S(2)}) collective-permute-start(bf16[112,960]{1,0:T(8,128)(2,1)} %collective-permute-done.25), channel_id=1, source_target_pairs={{0,1},{1,0},{2,3},{3,2},{4,5},{5,4},{6,7},{7,6},{8,9},{9,8},{10,11... | collective-permute-start | bytes 645128 | tf_op jit(solution)/shard_map/ppermute | solution.py:30
  87.6 148.7 %collective-permute-start.32 = (bf16[128,960]{0,1:T(8,128)(2,1)}, bf16[128,960]{0,1:T(8,128)(2,1)}, u32[]{:S(2)}, u32[]{:S(2)}) collective-permute-start(bf16[128,960]{0,1:T(8,128)(2,1)} %bitcast.67), channel_id=1, source_target_pairs={{0,2},{2,0},{1,3},{3,1},{4,6},{6,4},{5,7},{7,5},{8,10},{10,8},{9,1... | collective-permute-start | bytes 737288 | tf_op jit(solution)/shard_map/ppermute | solution.py:30
  91.9 19.0 %collective-permute-start.21 = (bf16[4,128,320]{1,2,0:T(8,128)(2,1)S(1)}, bf16[4,128,320]{1,2,0:T(8,128)(2,1)S(1)}, u32[]{:S(2)}, u32[]{:S(2)}) collective-permute-start(bf16[4,128,320]{1,2,0:T(8,128)(2,1)S(1)} %slice.657), channel_id=1, source_target_pairs={{0,16},{16,32},{32,48},{48,0},{1,17},{17,33},{33,49},{49,1},{2,18}... | collective-permute-start | bytes 983048 | tf_op jit(solution)/shard_map/ppermute | solution.py:30
  93.0 18.6 %collective-permute-start.22 = (bf16[4,128,320]{1,2,0:T(8,128)(2,1)S(1)}, bf16[4,128,320]{1,2,0:T(8,128)(2,1)S(1)}, u32[]{:S(2)}, u32[]{:S(2)}) collective-permute-start(bf16[4,128,320]{1,2,0:T(8,128)(2,1)S(1)} %slice.658), channel_id=1, source_target_pairs={{0,48},{16,0},{32,16},{48,32},{1,49},{17,1},{33,17},{49,33},{2,50}... | collective-permute-start | bytes 983048 | tf_op jit(solution)/shard_map/ppermute | solution.py:30
  98.0 84.4 %collective-permute-start.12 = (bf16[4,128,320]{1,2,0:T(8,128)(2,1)}, bf16[4,128,320]{1,2,0:T(8,128)(2,1)}, u32[]{:S(2)}, u32[]{:S(2)}) collective-permute-start(bf16[4,128,320]{1,2,0:T(8,128)(2,1)} %slice.650), channel_id=1, source_target_pairs={{0,4},{4,8},{8,12},{12,0},{1,5},{5,9},{9,13},{13,1},{2,6},{6,10},{... | collective-permute-start | bytes 983048 | tf_op jit(solution)/shard_map/ppermute | solution.py:30
  99.7 84.4 %collective-permute-start.13 = (bf16[4,128,320]{1,2,0:T(8,128)(2,1)}, bf16[4,128,320]{1,2,0:T(8,128)(2,1)}, u32[]{:S(2)}, u32[]{:S(2)}) collective-permute-start(bf16[4,128,320]{1,2,0:T(8,128)(2,1)} %slice.651), channel_id=1, source_target_pairs={{0,12},{4,0},{8,4},{12,8},{1,13},{5,1},{9,5},{13,9},{2,14},{6,2},{... | collective-permute-start | bytes 983048 | tf_op jit(solution)/shard_map/ppermute | solution.py:30
  244.9 252.4 %collective-permute-start.93 = (bf16[240,128]{1,0:T(8,128)(2,1)}, bf16[240,128]{1,0:T(8,128)(2,1)}, u32[]{:S(2)}, u32[]{:S(2)}) collective-permute-start(bf16[240,128]{1,0:T(8,128)(2,1)} %get-tuple-element.613), channel_id=1, source_target_pairs={{0,3},{1,2},{2,1},{3,0},{4,7},{5,6},{6,5},{7,4},{8,11},{9,10},{10,... | collective-permute-start | bytes 184328 | tf_op jit(solution)/shard_map/ppermute | solution.py:391
  257.9 22.4 %collective-permute-start.34 = (bf16[2,128,960]{1,2,0:T(8,128)(2,1)S(1)}, bf16[2,128,960]{1,2,0:T(8,128)(2,1)S(1)}, u32[]{:S(2)}, u32[]{:S(2)}) collective-permute-start(bf16[2,128,960]{1,2,0:T(8,128)(2,1)S(1)} %bitcast.849), channel_id=1, source_target_pairs={{0,2},{2,0},{1,3},{3,1},{4,6},{6,4},{5,7},{7,5},{8,10},{10,8},{9,1... | collective-permute-start | bytes 1474568 | tf_op jit(solution)/shard_map/ppermute | solution.py:30
  259.2 22.7 %collective-permute-start.30 = (bf16[2,128,960]{1,2,0:T(8,128)(2,1)S(1)}, bf16[2,128,960]{1,2,0:T(8,128)(2,1)S(1)}, u32[]{:S(2)}, u32[]{:S(2)}) collective-permute-start(bf16[2,128,960]{1,2,0:T(8,128)(2,1)S(1)} %bitcast.848), channel_id=1, source_target_pairs={{0,2},{2,0},{1,3},{3,1},{4,6},{6,4},{5,7},{7,5},{8,10},{10,8},{9,1... | collective-permute-start | bytes 1474568 | tf_op jit(solution)/shard_map/ppermute | solution.py:30
  275.4 136.4 %collective-permute-start.129 = (bf16[4,96,640]{2,1,0:T(8,128)(2,1)}, bf16[4,96,640]{2,1,0:T(8,128)(2,1)}, u32[]{:S(2)}, u32[]{:S(2)}) collective-permute-start(bf16[4,96,640]{2,1,0:T(8,128)(2,1)} %pad_maximum_fusion.17), channel_id=1, source_target_pairs={{0,12},{4,0},{8,4},{12,8},{1,13},{5,1},{9,5},{13,9},{2,14},{6,2},{... | collective-permute-start | bytes 1474568 | tf_op jit(solution)/shard_map/ppermute | solution.py:30
  279.0 132.8 %collective-permute-start.127 = (bf16[4,96,640]{2,1,0:T(8,128)(2,1)}, bf16[4,96,640]{2,1,0:T(8,128)(2,1)}, u32[]{:S(2)}, u32[]{:S(2)}) collective-permute-start(bf16[4,96,640]{2,1,0:T(8,128)(2,1)} %pad_maximum_fusion.16), channel_id=1, source_target_pairs={{0,4},{4,8},{8,12},{12,0},{1,5},{5,9},{9,13},{13,1},{2,6},{6,10},{... | collective-permute-start | bytes 1474568 | tf_op jit(solution)/shard_map/ppermute | solution.py:30
  280.3 139.3 %collective-permute-start.114 = (bf16[4,96,640]{2,1,0:T(8,128)(2,1)}, bf16[4,96,640]{2,1,0:T(8,128)(2,1)}, u32[]{:S(2)}, u32[]{:S(2)}) collective-permute-start(bf16[4,96,640]{2,1,0:T(8,128)(2,1)} %pad_maximum_fusion.15), channel_id=1, source_target_pairs={{0,48},{16,0},{32,16},{48,32},{1,49},{17,1},{33,17},{49,33},{2,50}... | collective-permute-start | bytes 1474568 | tf_op jit(solution)/shard_map/ppermute | solution.py:30
  283.6 137.0 %collective-permute-start.112 = (bf16[4,96,640]{2,1,0:T(8,128)(2,1)}, bf16[4,96,640]{2,1,0:T(8,128)(2,1)}, u32[]{:S(2)}, u32[]{:S(2)}) collective-permute-start(bf16[4,96,640]{2,1,0:T(8,128)(2,1)} %pad_maximum_fusion.14), channel_id=1, source_target_pairs={{0,16},{16,32},{32,48},{48,0},{1,17},{17,33},{33,49},{49,1},{2,18}... | collective-permute-start | bytes 1474568 | tf_op jit(solution)/shard_map/ppermute | solution.py:30
  414.5 27.6 %collective-permute-start.132 = (bf16[96,640]{1,0:T(8,128)(2,1)}, bf16[96,640]{1,0:T(8,128)(2,1)}, u32[]{:S(2)}, u32[]{:S(2)}) collective-permute-start(bf16[96,640]{1,0:T(8,128)(2,1)} %get-tuple-element.580), channel_id=1, source_target_pairs={{0,32},{16,48},{32,0},{48,16},{1,33},{17,49},{33,1},{49,17},{2,34}... | collective-permute-start | bytes 368648 | tf_op jit(solution)/shard_map/ppermute | solution.py:30
  415.5 28.0 %collective-permute-start.131 = (bf16[96,640]{1,0:T(8,128)(2,1)}, bf16[96,640]{1,0:T(8,128)(2,1)}, u32[]{:S(2)}, u32[]{:S(2)}) collective-permute-start(bf16[96,640]{1,0:T(8,128)(2,1)} %get-tuple-element.581), channel_id=1, source_target_pairs={{0,16},{16,32},{32,48},{48,0},{1,17},{17,33},{33,49},{49,1},{2,18}... | collective-permute-start | bytes 368648 | tf_op jit(solution)/shard_map/ppermute | solution.py:30
  419.6 26.4 %collective-permute-start.130 = (bf16[96,640]{1,0:T(8,128)(2,1)}, bf16[96,640]{1,0:T(8,128)(2,1)}, u32[]{:S(2)}, u32[]{:S(2)}) collective-permute-start(bf16[96,640]{1,0:T(8,128)(2,1)} %get-tuple-element.579), channel_id=1, source_target_pairs={{0,48},{16,0},{32,16},{48,32},{1,49},{17,1},{33,17},{49,33},{2,50}... | collective-permute-start | bytes 368648 | tf_op jit(solution)/shard_map/ppermute | solution.py:30
  449.0 51.6 %collective-permute-start.92 = (bf16[240,128]{1,0:T(8,128)(2,1)}, bf16[240,128]{1,0:T(8,128)(2,1)S(1)}, u32[]{:S(2)}, u32[]{:S(2)}) collective-permute-start(bf16[240,128]{1,0:T(8,128)(2,1)} %get-tuple-element.614), channel_id=1, source_target_pairs={{0,2},{1,3},{2,0},{3,1},{4,6},{5,7},{6,4},{7,5},{8,10},{9,11},{10,... | collective-permute-start | bytes 184328 | tf_op jit(solution)/shard_map/ppermute | solution.py:391
  451.3 19.3 %collective-permute-start.47 = (bf16[4,128,320]{1,2,0:T(8,128)(2,1)}, bf16[4,128,320]{1,2,0:T(8,128)(2,1)S(1)}, u32[]{:S(2)}, u32[]{:S(2)}) collective-permute-start(bf16[4,128,320]{1,2,0:T(8,128)(2,1)} %get-tuple-element.533), channel_id=1, source_target_pairs={{0,12},{4,0},{8,4},{12,8},{1,13},{5,1},{9,5},{13,9},{2,14},{6,2},{... | collective-permute-start | bytes 983048 | tf_op jit(solution)/shard_map/ppermute | solution.py:30
  491.6 34.9 %collective-permute-start.58 = (bf16[2,128,960]{1,2,0:T(8,128)(2,1)S(1)}, bf16[2,128,960]{1,2,0:T(8,128)(2,1)S(1)}, u32[]{:S(2)}, u32[]{:S(2)}) collective-permute-start(bf16[2,128,960]{1,2,0:T(8,128)(2,1)S(1)} %pad_maximum_fusion.12), channel_id=1, source_target_pairs={{0,1},{1,0},{2,3},{3,2},{4,5},{5,4},{6,7},{7,6},{8,9},{9,8},{10,11... | collective-permute-start | bytes 1474568 | tf_op jit(solution)/shard_map/ppermute | solution.py:30
  497.2 30.3 %collective-permute-start.137 = (bf16[1,4,96,640]{3,2,1,0:T(8,128)(2,1)S(1)}, bf16[1,4,96,640]{3,2,1,0:T(8,128)(2,1)S(1)}, u32[]{:S(2)}, u32[]{:S(2)}) collective-permute-start(bf16[1,4,96,640]{3,2,1,0:T(8,128)(2,1)S(1)} %bitcast_dynamic-update-slice_fusion.4), channel_id=1, source_target_pairs={{0,4},{4,8},{8,12},{12,0},{1,5},{5,9},{9,13},{13,1},{2,6},{6,10},{... | collective-permute-start | bytes 1474568 | tf_op jit(solution)/shard_map/ppermute | solution.py:30
  497.4 31.3 %collective-permute-start.138 = (bf16[1,4,96,640]{3,2,1,0:T(8,128)(2,1)S(1)}, bf16[1,4,96,640]{3,2,1,0:T(8,128)(2,1)S(1)}, u32[]{:S(2)}, u32[]{:S(2)}) collective-permute-start(bf16[1,4,96,640]{3,2,1,0:T(8,128)(2,1)S(1)} %bitcast_dynamic-update-slice_fusion.4), channel_id=1, source_target_pairs={{0,12},{4,0},{8,4},{12,8},{1,13},{5,1},{9,5},{13,9},{2,14},{6,2},{... | collective-permute-start | bytes 1474568 | tf_op jit(solution)/shard_map/ppermute | solution.py:30
  526.6 21.1 %collective-permute-start.48 = (bf16[8,128,320]{1,2,0:T(8,128)(2,1)S(1)}, bf16[8,128,320]{1,2,0:T(8,128)(2,1)S(1)}, u32[]{:S(2)}, u32[]{:S(2)}) collective-permute-start(bf16[8,128,320]{1,2,0:T(8,128)(2,1)S(1)} %pad_maximum_fusion.6), channel_id=1, source_target_pairs={{0,12},{4,0},{8,4},{12,8},{1,13},{5,1},{9,5},{13,9},{2,14},{6,2},{... | collective-permute-start | bytes 1966088 | tf_op jit(solution)/shard_map/ppermute | solution.py:30
  527.5 21.1 %collective-permute-start.46 = (bf16[8,128,320]{1,2,0:T(8,128)(2,1)S(1)}, bf16[8,128,320]{1,2,0:T(8,128)(2,1)S(1)}, u32[]{:S(2)}, u32[]{:S(2)}) collective-permute-start(bf16[8,128,320]{1,2,0:T(8,128)(2,1)S(1)} %pad_maximum_fusion.5), channel_id=1, source_target_pairs={{0,4},{4,8},{8,12},{12,0},{1,5},{5,9},{9,13},{13,1},{2,6},{6,10},{... | collective-permute-start | bytes 1966088 | tf_op jit(solution)/shard_map/ppermute | solution.py:30
  547.7 71.8 %collective-permute-start.31 = (bf16[128,960]{0,1:T(8,128)(2,1)S(1)}, bf16[128,960]{0,1:T(8,128)(2,1)S(1)}, u32[]{:S(2)}, u32[]{:S(2)}) collective-permute-start(bf16[128,960]{0,1:T(8,128)(2,1)S(1)} %copy-done.47), channel_id=1, source_target_pairs={{0,1},{1,0},{2,3},{3,2},{4,5},{5,4},{6,7},{7,6},{8,9},{9,8},{10,11... | collective-permute-start | bytes 737288 | tf_op jit(solution)/shard_map/ppermute | solution.py:30
  547.7 30.7 %collective-permute-start.139 = (bf16[1,2,96,640]{3,2,1,0:T(8,128)(2,1)S(1)}, bf16[1,2,96,640]{3,2,1,0:T(8,128)(2,1)S(1)}, u32[]{:S(2)}, u32[]{:S(2)}) collective-permute-start(bf16[1,2,96,640]{3,2,1,0:T(8,128)(2,1)S(1)} %slice.735), channel_id=1, source_target_pairs={{0,4},{4,8},{8,12},{12,0},{1,5},{5,9},{9,13},{13,1},{2,6},{6,10},{... | collective-permute-start | bytes 737288 | tf_op jit(solution)/shard_map/ppermute | solution.py:30
  584.2 25.9 %collective-permute-start.52 = (bf16[2,128,320]{1,2,0:T(8,128)(2,1)S(1)}, bf16[2,128,320]{1,2,0:T(8,128)(2,1)S(1)}, u32[]{:S(2)}, u32[]{:S(2)}) collective-permute-start(bf16[2,128,320]{1,2,0:T(8,128)(2,1)S(1)} %pad_maximum_fusion.27), channel_id=1, source_target_pairs={{0,48},{16,0},{32,16},{48,32},{1,49},{17,1},{33,17},{49,33},{2,50}... | collective-permute-start | bytes 491528 | tf_op jit(solution)/shard_map/ppermute | solution.py:30
  584.2 25.9 %collective-permute-start.50 = (bf16[2,128,320]{1,2,0:T(8,128)(2,1)S(1)}, bf16[2,128,320]{1,2,0:T(8,128)(2,1)S(1)}, u32[]{:S(2)}, u32[]{:S(2)}) collective-permute-start(bf16[2,128,320]{1,2,0:T(8,128)(2,1)S(1)} %pad_maximum_fusion.26), channel_id=1, source_target_pairs={{0,16},{16,32},{32,48},{48,0},{1,17},{17,33},{33,49},{49,1},{2,18}... | collective-permute-start | bytes 491528 | tf_op jit(solution)/shard_map/ppermute | solution.py:30
  (197 other events, 2264.8 us)
